TPU v7x, 32 devices: a whole 2x2x4 slice. The times are simulated.
32 devices in a mesh: tm: 8 (over z, x), wafer: 4 (over y, core).
Axes of the slice: x: 2, y: 2, z: 4, core: 2. Of those that a mesh axis runs over, the one named last changes fastest.
Arguments:
- timestream: bfloat16 [1024, 32768], P('wafer', 'tm'), may hold values from -6 to 6
- sample_weight: bfloat16 [1024, 32768], P('wafer', 'tm'), may hold values from 0 to 4
- response: float32 [3, 1024], replicated, may hold values from -1 to 1
- band_filter: bfloat16 [256, 256], replicated, may hold values from -0.375 to 0.375
- whiten: bfloat16 [7, 1024, 1024], P(None, ('tm', 'wafer')), as said below
- group_wafer: int32 [8], replicated, may hold values from 0 to 6
- pointing: bfloat16 [128, 6, 256, 256], P(('tm', 'wafer')), may hold values from -0.15625 to 0.15625
- tile_list: int32 [128, 6], P(('tm', 'wafer')), may hold values from 0 to 255, as said below
- tile_home: int32 [256], replicated, may hold values from 0 to 255, as said below
- solution: float32 [256, 3, 256], P('tm'), may hold values from -6 to 6
- direction: float32 [256, 3, 256], P('tm'), may hold values from -6 to 6
- cg_scalars: float32 [2], replicated, may hold values from 0.5 to 1.5
Outputs:
- solution_next: float32 [256, 3, 256], P('tm')
- residual_next: float32 [256, 3, 256], P('tm')
- direction_next: float32 [256, 3, 256], P('tm')
Inputs may be any that keep to these rules, and one draw needn't show every extreme that they name: `tile_list`: the tiles named in the spans of one device (one index of tm and one of wafer) are all different; among them at most 3 have their row tile_home on one index of tm, and in every draw, for each index of wafer, some index of tm owns exactly 3 tiles named by every device of that wafer index. A permutation: row tile_home[i] of a map holds sky tile i. `whiten`: each whitening matrix is symmetric.
All inputs are finite; a program needn't handle non-finite values.
Results may differ from a plain program's by a relative error of at most 0.0033.
The roundings to bfloat16 on the way count: a program that leaves them out, or rounds other values in their place, can miss the bound.
Values may be sent and summed in bfloat16 or wider, within the bound.
A program may use at most 128 MiB of HBM per device.

v0:
```python
import jax
import jax.numpy as jnp
from jax import lax
from jax.sharding import PartitionSpec as P


def shards(
    timestream,
    sample_weight,
    response,
    band_filter,
    whiten,
    group_wafer,
    pointing,
    tile_list,
    tile_home,
    solution,
    direction,
    cg_scalars,
):
    precise_mode = lax.Precision.HIGHEST
    tm_count = lax.axis_size("tm")
    tm_index = lax.axis_index("tm")
    step_size = cg_scalars[0]
    blend_weight = cg_scalars[1]
    updated = solution + step_size * direction
    short_map = updated.astype(jnp.bfloat16)
    tiles_own, comp_count, pixel_count = solution.shape
    spans_here, per_span = tile_list.shape
    samples = band_filter.shape[0]
    det_total = whiten.shape[2]
    row_count = spans_here * per_span
    capacity = max(2, (row_count + tm_count - 1) // tm_count)
    tile_ids = tile_list.reshape(row_count)
    home_rows = jnp.take(tile_home, tile_ids, axis=0)
    owners = home_rows // tiles_own
    local_slot = home_rows % tiles_own
    positions = jnp.arange(row_count, dtype=jnp.int32)
    earlier = (owners[:, None] == owners[None, :]) & (positions[None, :] < positions[:, None])
    before_count = jnp.sum(earlier.astype(jnp.int32), axis=1)
    targets = owners * capacity + before_count
    placing = targets[:, None] == jnp.arange(tm_count * capacity, dtype=jnp.int32)[None, :]
    requests = jnp.sum(jnp.where(placing, local_slot[:, None], 0), axis=0)
    requests = requests.reshape(tm_count, capacity)
    asked_slots = lax.all_to_all(requests, "tm", split_axis=0, concat_axis=0, tiled=True)
    served = jnp.take(short_map, asked_slots, axis=0)
    replies, asked_slots = (
        lax.all_to_all(served, "tm", split_axis=0, concat_axis=0, tiled=True),
        asked_slots,
    )
    fetched = jnp.take(
        replies.reshape(tm_count * capacity, comp_count, pixel_count), targets, axis=0
    )
    fetched = fetched.reshape(spans_here, per_span, comp_count, pixel_count)
    signal_parts = jnp.einsum(
        "cktp,ckjp->cjt", pointing, fetched, preferred_element_type=jnp.float32
    )
    wafer_pick = group_wafer[tm_index]
    matrix = lax.dynamic_index_in_dim(
        lax.all_gather(whiten, ("tm", "wafer"), axis=1, tiled=True), wafer_pick, 0, keepdims=False
    )
    columns, column_weights = (
        lax.all_to_all(timestream, "wafer", split_axis=1, concat_axis=0, tiled=True),
        lax.all_to_all(sample_weight, "wafer", split_axis=1, concat_axis=0, tiled=True),
    )
    column_weights = column_weights.astype(jnp.float32).reshape(det_total, spans_here, samples)
    signal = jnp.einsum("jd,cjt->dct", response, signal_parts, precision=precise_mode)
    errors = (
        (columns.astype(jnp.float32).reshape(det_total, spans_here, samples) - signal)
        * column_weights
    ).astype(jnp.bfloat16)
    filtered = jnp.dot(
        errors.reshape(det_total * spans_here, samples),
        band_filter,
        preferred_element_type=jnp.float32,
    )
    filtered = filtered.astype(jnp.bfloat16).reshape(det_total, spans_here * samples)
    whitened = jnp.dot(matrix, filtered, preferred_element_type=jnp.float32).astype(jnp.bfloat16)
    smoothed = lax.dot_general(
        whitened.reshape(det_total * spans_here, samples),
        band_filter,
        (((1,), (1,)), ((), ())),
        preferred_element_type=jnp.float32,
    )
    smoothed = smoothed.astype(jnp.bfloat16).reshape(det_total, spans_here, samples)
    stokes = jnp.einsum(
        "jd,dct->cjt",
        response,
        smoothed.astype(jnp.float32) * column_weights,
        precision=precise_mode,
    )
    stokes_short = stokes.astype(jnp.bfloat16)
    partial_value = jnp.einsum(
        "cjt,cktp->ckjp", stokes_short, pointing, preferred_element_type=jnp.float32
    )
    partial_value = partial_value.reshape(row_count, comp_count * pixel_count)
    outgoing = jnp.dot(placing.astype(jnp.float32).T, partial_value, precision=precise_mode)
    outgoing = outgoing.reshape(tm_count, capacity, comp_count, pixel_count)
    arrived = lax.all_to_all(outgoing, "tm", split_axis=0, concat_axis=0, tiled=True)
    slot_hits = (
        asked_slots.reshape(-1)[None, :] == jnp.arange(tiles_own, dtype=jnp.int32)[:, None]
    ).astype(jnp.float32)
    owned_sum = jnp.dot(
        slot_hits,
        arrived.reshape(tm_count * capacity, comp_count * pixel_count),
        precision=precise_mode,
    )
    owned_sum = owned_sum.reshape(tiles_own, comp_count, pixel_count)
    summed = lax.psum(owned_sum, "wafer")
    residual_next = summed * float(det_total) ** (-0.5)
    direction_next = residual_next + blend_weight * direction
    return (updated, residual_next, direction_next)


def solution(mesh):
    in_specs = (
        P("wafer", "tm"),
        P("wafer", "tm"),
        P(),
        P(),
        P(None, ("tm", "wafer"), None),
        P(),
        P(("tm", "wafer"), None, None, None),
        P(("tm", "wafer"), None),
        P(),
        P("tm", None, None),
        P("tm", None, None),
        P(),
    )
    out_specs = (P("tm", None, None), P("tm", None, None), P("tm", None, None))
    return jax.shard_map(shards, mesh=mesh, in_specs=in_specs, out_specs=out_specs, check_vma=False)
```

profile of v0, /device:TPU:1, one launch (start us, length us, event | category | flops | bytes accessed | tf_op | source)
XLA Modules:
  0.0 243.1 jit_solution(12261012221184086792)
XLA Ops:
  7.2 0.7 all-gather.2.cloned.1.call-update
  7.9 1.0 reshape.319
  8.9 0.8 reshape.318
  9.7 1.4 gather_fusion
  11.3 0.7 all_to_all.36
  12.0 6.4 %all-to-all-start = ((s32[8,1,3]{2,1,0:T(1,128)}), s32[8,1,3]{2,1,0:T(1,128)S(1)}, u32[]{:S(2)}, u32[]{:S(2)}) async-start(s32[8,1,3]{2,1,0:T(1,128)} %bitcast.2), calls=%async_computation | async-start | bytes 8192 | tf_op jit(solution)/shard_map/all_to_all | solution.py:45
  18.4 1.4 fusion.41
  19.8 1.7 fusion.40
  21.5 2.1 all-to-all-done
  24.1 0.6 gather_fusion.1
  24.8 0.6 copy.72
  25.4 3.3 %all-to-all-start.2 = ((bf16[8,3,3,256]{3,1,2,0:T(4,128)(2,1)}), bf16[8,3,3,256]{3,1,2,0:T(4,128)(2,1)S(1)}, u32[]{:S(2)}, u32[]{:S(2)}) async-start(bf16[8,3,3,256]{3,1,2,0:T(4,128)(2,1)} %copy.72), calls=%async_computation.2 | async-start | bytes 98304 | tf_op jit(solution)/shard_map/all_to_all | solution.py:48
  28.8 4.1 %copy.77 = bf16[256,4096]{0,1:T(8,128)(2,1)} copy(bf16[256,4096]{1,0:T(8,128)(2,1)} %param.13) | data formatting | bytes 4194304 | tf_op args[1]
  32.9 1.9 all-to-all-done.2
  34.8 7.8 %all-to-all-start.3 = ((bf16[256,4,1024]{0,2,1:T(8,128)(2,1)}), bf16[256,4,1024]{0,2,1:T(8,128)(2,1)}, u32[]{:S(2)}, u32[]{:S(2)}) async-start(bf16[256,4,1024]{0,2,1:T(8,128)(2,1)} %bitcast.106), calls=%async_computation.3 | async-start | bytes 4194304 | tf_op jit(solution)/shard_map/all_to_all | solution.py:64
  42.6 4.1 %copy.65 = bf16[256,4096]{0,1:T(8,128)(2,1)} copy(bf16[256,4096]{1,0:T(8,128)(2,1)} %param.12) | data formatting | bytes 4194304 | tf_op args[0]
  46.8 26.4 %all-to-all-done.3 = bf16[256,4,1024]{0,2,1:T(8,128)(2,1)} async-done(((bf16[256,4,1024]{0,2,1:T(8,128)(2,1)}), bf16[256,4,1024]{0,2,1:T(8,128)(2,1)}, u32[]{:S(2)}, u32[]{:S(2)}) %all-to-all-start.3) | async-done | bytes 2097184 | tf_op jit(solution)/shard_map/all_to_all | solution.py:64
  73.2 5.1 %all-to-all-start.1 = ((bf16[256,4,1024]{0,2,1:T(8,128)(2,1)}), bf16[256,4,1024]{0,2,1:T(8,128)(2,1)}, u32[]{:S(2)}, u32[]{:S(2)}) async-start(bf16[256,4,1024]{0,2,1:T(8,128)(2,1)} %bitcast.105), calls=%async_computation.1 | async-start | bytes 4194304 | tf_op jit(solution)/shard_map/all_to_all | solution.py:63
  78.4 0.6 dynamic_slice.7
  81.0 0.6 gather_fusion.2
  81.7 0.9 convolution_bitcast_fusion
  82.6 2.0 convert_bitcast_fusion
  84.6 4.7 %copy.78 = f32[4,256,1024]{1,0,2:T(4,128)} copy(f32[4,256,1024]{1,2,0:T(8,128)S(1)} %convert_bitcast_fusion) | data formatting | bytes 8388608 | tf_op jit(solution)/shard_map/convert_element_type | solution.py:66
  89.3 5.8 %reshape.327 = f32[1024,4,256]{0,2,1:T(8,128)} reshape(f32[4,256,1024]{1,0,2:T(4,128)} %copy.78) | data formatting | bytes 8388608 | tf_op jit(solution)/shard_map/convert_element_type | solution.py:66
  95.1 28.7 %all-to-all-done.1 = bf16[256,4,1024]{0,2,1:T(8,128)(2,1)} async-done(((bf16[256,4,1024]{0,2,1:T(8,128)(2,1)}), bf16[256,4,1024]{0,2,1:T(8,128)(2,1)}, u32[]{:S(2)}, u32[]{:S(2)}) %all-to-all-start.1) | async-done | bytes 2097184 | tf_op jit(solution)/shard_map/all_to_all | solution.py:63
  123.8 2.0 convert_bitcast_fusion.1
  125.8 4.7 %copy.66 = f32[4,256,1024]{1,0,2:T(4,128)} copy(f32[4,256,1024]{1,2,0:T(8,128)S(1)} %convert_bitcast_fusion.1) | data formatting | bytes 8388608 | tf_op jit(solution)/shard_map/convert_element_type | solution.py:69
  130.5 6.1 %reshape.326 = f32[1024,4,256]{0,2,1:T(8,128)} reshape(f32[4,256,1024]{1,0,2:T(4,128)} %copy.66) | data formatting | bytes 8388608 | tf_op jit(solution)/shard_map/convert_element_type | solution.py:69
  136.6 7.1 %fusion.2 = bf16[1024,4,256]{0,2,1:T(8,128)(2,1)} fusion(f32[1024,4,256]{0,2,1:T(8,128)} %reshape.327, f32[1024,4,256]{0,2,1:T(8,128)} %reshape.326, f32[4,3,256]{2,1,0:T(4,128)S(1)} %convolution_bitcast_fusion, f32[3,1024]{1,0:T(4,128)S(1)} %copy-done.3), kind=kOutput, calls=%fused_computation.8 | convolution fusion | flops 40894464 | bytes 10510336 | tf_op jit(solution)/shard_map/jd,cjt->dct/dot_general | solution.py:67
  143.6 4.2 %copy.79 = bf16[1024,4,256]{2,1,0:T(4,128)(2,1)} copy(bf16[1024,4,256]{0,2,1:T(8,128)(2,1)} %fusion.2) | data formatting | bytes 4194304 | tf_op jit(solution)/shard_map/convert_element_type | solution.py:71
  147.9 4.0 %reshape.321 = bf16[4096,256]{1,0:T(8,128)(2,1)} reshape(bf16[1024,4,256]{2,1,0:T(4,128)(2,1)} %copy.79) | data formatting | bytes 4194304 | tf_op jit(solution)/shard_map/reshape | solution.py:73
  151.9 3.6 %convolution_convert_fusion.1 = bf16[4096,256]{1,0:T(8,128)(2,1)} fusion(bf16[4096,256]{1,0:T(8,128)(2,1)} %reshape.321, bf16[256,256]{1,0:T(8,128)(2,1)S(1)} %copy-done.1), kind=kOutput, calls=%fused_computation.5 | convolution fusion | flops 537919488 | bytes 4325376 | tf_op jit(solution)/shard_map/dot_general | solution.py:72
  155.5 4.4 %reshape.322 = bf16[1024,1024]{1,0:T(8,128)(2,1)} reshape(bf16[4096,256]{1,0:T(8,128)(2,1)} %convolution_convert_fusion.1) | data formatting | bytes 4194304 | tf_op jit(solution)/shard_map/reshape | solution.py:77
  159.9 5.9 %fusion.8 = bf16[1024,1024]{1,0:T(8,128)(2,1)} fusion(bf16[1024,1024]{1,0:T(8,128)(2,1)} %reshape.322, bf16[7,1024,1024]{2,1,0:T(8,128)(2,1)} %all-gather.2.cloned.1.call-done, s32[]{:T(128)S(6)} %select_n.167), kind=kOutput, calls=%fused_computation.16 | convolution fusion | flops 2148532224 | bytes 6291460 | tf_op jit(solution)/shard_map/dot_general | solution.py:78
  165.8 4.4 %reshape.323 = bf16[4096,256]{1,0:T(8,128)(2,1)} reshape(bf16[1024,1024]{1,0:T(8,128)(2,1)} %fusion.8) | data formatting | bytes 4194304 | tf_op jit(solution)/shard_map/reshape | solution.py:80
  170.1 4.3 %fusion = f32[4096,256]{1,0:T(8,128)} fusion(bf16[4096,256]{1,0:T(8,128)(2,1)} %reshape.323, bf16[256,256]{1,0:T(8,128)(2,1)S(1)} %copy-done.1), kind=kOutput, calls=%fused_computation.4 | convolution fusion | flops 538968064 | bytes 6422528 | tf_op jit(solution)/shard_map/dot_general | solution.py:79
  174.4 5.2 %reshape.328 = f32[1024,4,256]{2,1,0:T(4,128)} reshape(f32[4096,256]{1,0:T(8,128)} %fusion) | data formatting | bytes 8388608 | tf_op jit(solution)/shard_map/convert_element_type | solution.py:89
  179.6 5.3 %copy.80 = f32[1024,4,256]{0,2,1:T(8,128)} copy(f32[1024,4,256]{2,1,0:T(4,128)} %reshape.328) | data formatting | bytes 8388608 | tf_op jit(solution)/shard_map/convert_element_type | solution.py:89
  184.9 7.2 %fusion.14 = bf16[4,256,3,1]{1,2,3,0:T(4,128)(2,1)S(1)} fusion(f32[1024,4,256]{0,2,1:T(8,128)} %copy.80, f32[1024,4,256]{0,2,1:T(8,128)} %reshape.327, f32[3,1024]{1,0:T(4,128)S(1)} %copy-done.3), kind=kOutput, calls=%fused_computation.19 | convolution fusion | flops 38800384 | bytes 8407040 | tf_op jit(solution)/shard_map/jd,dct->cjt/dot_general | solution.py:86
  192.1 0.5 fusion.42
  192.8 0.7 copy.83
  193.5 5.3 %all-to-all-start.4 = ((f32[8,3,3,256]{3,2,1,0:T(4,128)}), f32[8,3,3,256]{3,2,1,0:T(4,128)S(1)}, u32[]{:S(2)}, u32[]{:S(2)}) async-start(f32[8,3,3,256]{3,2,1,0:T(4,128)} %copy.83), calls=%async_computation.4 | async-start | bytes 196608 | tf_op jit(solution)/shard_map/all_to_all | solution.py:99
  199.4 0.7 reduce.3
  200.1 4.8 %all-to-all-done.4 = f32[8,3,3,256]{3,2,1,0:T(4,128)S(1)} async-done(((f32[8,3,3,256]{3,2,1,0:T(4,128)}), f32[8,3,3,256]{3,2,1,0:T(4,128)S(1)}, u32[]{:S(2)}, u32[]{:S(2)}) %all-to-all-start.4) | async-done | bytes 73760 | tf_op jit(solution)/shard_map/all_to_all | solution.py:99
  204.9 1.0 fusion.17
  205.9 0.7 copy.85
  206.5 27.5 %all-reduce.2.cloned.1.call-done = f32[32,3,256]{2,0,1:T(8,128)} async-done(((f32[32,3,256]{2,0,1:T(8,128)}), f32[32,3,256]{2,0,1:T(8,128)}) %all-reduce.2.cloned.1.call-update) | async-done | bytes 98320 | tf_op jit(solution)/shard_map/psum | solution.py:109
  234.0 2.3 multiply_add_fusion
  (42 shorter events, 2.1 us)
Async XLA Ops:
  7.2 74.6 %copy-start = (bf16[4,6,256,256]{3,2,1,0:T(8,128)(2,1)S(1)}, bf16[4,6,256,256]{3,2,1,0:T(8,128)(2,1)}, u32[]{:S(2)}) copy-start(bf16[4,6,256,256]{3,2,1,0:T(8,128)(2,1)} %param.18) | copy-start | bytes 9437188
  7.2 152.7 %all-gather.2.cloned.1.call-start = ((), (), s32[]{:S(2)}) async-start(), calls=%async_computation.5 | async-start | bytes 15138816 | tf_op jit(solution)/shard_map/all_gather | solution.py:60
  12.0 11.6 %all-to-all-start = ((s32[8,1,3]{2,1,0:T(1,128)}), s32[8,1,3]{2,1,0:T(1,128)S(1)}, u32[]{:S(2)}, u32[]{:S(2)}) async-start(s32[8,1,3]{2,1,0:T(1,128)} %bitcast.2), calls=%async_computation | async-start | bytes 8192 | tf_op jit(solution)/shard_map/all_to_all | solution.py:45
  25.4 9.4 %all-to-all-start.2 = ((bf16[8,3,3,256]{3,1,2,0:T(4,128)(2,1)}), bf16[8,3,3,256]{3,1,2,0:T(4,128)(2,1)S(1)}, u32[]{:S(2)}, u32[]{:S(2)}) async-start(bf16[8,3,3,256]{3,1,2,0:T(4,128)(2,1)} %copy.72), calls=%async_computation.2 | async-start | bytes 98304 | tf_op jit(solution)/shard_map/all_to_all | solution.py:48
  34.8 38.4 %all-to-all-start.3 = ((bf16[256,4,1024]{0,2,1:T(8,128)(2,1)}), bf16[256,4,1024]{0,2,1:T(8,128)(2,1)}, u32[]{:S(2)}, u32[]{:S(2)}) async-start(bf16[256,4,1024]{0,2,1:T(8,128)(2,1)} %bitcast.106), calls=%async_computation.3 | async-start | bytes 4194304 | tf_op jit(solution)/shard_map/all_to_all | solution.py:64
  46.8 31.6 %copy-start.5 = (s32[8]{0:T(128)S(1)}, s32[8]{0:T(128)}, u32[]{:S(2)}) copy-start(s32[8]{0:T(128)} %param.17) | copy-start | bytes 100
  46.8 34.2 %copy-start.4 = (s32[4,6]{1,0:T(4,128)S(1)}, s32[4,6]{1,0:T(4,128)}, u32[]{:S(2)}) copy-start(s32[4,6]{1,0:T(4,128)} %param.19) | copy-start | bytes 292
  73.2 50.7 %all-to-all-start.1 = ((bf16[256,4,1024]{0,2,1:T(8,128)(2,1)}), bf16[256,4,1024]{0,2,1:T(8,128)(2,1)}, u32[]{:S(2)}, u32[]{:S(2)}) async-start(bf16[256,4,1024]{0,2,1:T(8,128)(2,1)} %bitcast.105), calls=%async_computation.1 | async-start | bytes 4194304 | tf_op jit(solution)/shard_map/all_to_all | solution.py:63
  130.5 6.1 %copy-start.3 = (f32[3,1024]{1,0:T(4,128)S(1)}, f32[3,1024]{1,0:T(4,128)}, u32[]{:S(2)}) copy-start(f32[3,1024]{1,0:T(4,128)} %param.14) | copy-start | bytes 36868
  147.9 4.0 %copy-start.1 = (bf16[256,256]{1,0:T(8,128)(2,1)S(1)}, bf16[256,256]{1,0:T(8,128)(2,1)}, u32[]{:S(2)}) copy-start(bf16[256,256]{1,0:T(8,128)(2,1)} %param.15) | copy-start | bytes 393220
  192.1 41.9 %copy-start.2 = (f32[32,3,256]{2,0,1:T(8,128)S(1)}, f32[32,3,256]{2,0,1:T(8,128)}, u32[]{:S(2)}) copy-start(f32[32,3,256]{2,0,1:T(8,128)} %param.22) | copy-start | bytes 294916
  193.5 11.4 %all-to-all-start.4 = ((f32[8,3,3,256]{3,2,1,0:T(4,128)}), f32[8,3,3,256]{3,2,1,0:T(4,128)S(1)}, u32[]{:S(2)}, u32[]{:S(2)}) async-start(f32[8,3,3,256]{3,2,1,0:T(4,128)} %copy.83), calls=%async_computation.4 | async-start | bytes 196608 | tf_op jit(solution)/shard_map/all_to_all | solution.py:99
  198.8 35.2 %all-reduce.2.cloned.1.call-start = ((), (), s32[]{:S(2)}) async-start(), calls=%async_computation.6 | async-start | bytes 196608 | tf_op jit(solution)/shard_map/psum | solution.py:109
Sparse Core Ops, SparseCore 0:
  11.0 129.8 all-gather.1
  206.0 27.9 all-reduce.1
where the time goes:
time: 247 us; the launch traced here: 243 us
  waiting for transfers between devices  92.1 us (37%)
  local copies, waits for them, and re-layouts  67.2 us (27%)
  matrix products  30.6 us (12%)
  starting transfers between devices  28 us (11%)
  between operations  16.1 us (7%)
  other arithmetic  9.14 us (4%)
    all_to_all x1, waiting for transfers between devices, shards(): lax.all_to_all(timestream, 'wafer', split_axis=1, concat_axis=0, tiled=True)  28.7 us
    psum x1, waiting for transfers between devices, shards(): summed = lax.psum(owned_sum, 'wafer')  27.5 us
    all_to_all x1, waiting for transfers between devices, shards(): lax.all_to_all(sample_weight, 'wafer', split_axis=1, concat_axis=0, tiled...  26.4 us
    convert_element_type x2, local copies, waits for them, and re-layouts, shards(): columns.astype(jnp.float32).reshape(det_total, spans_here, samples) - signal  10.8 us
    convert_element_type x2, local copies, waits for them, and re-layouts, shards(): column_weights.astype(jnp.float32).reshape(det_total, spans_here, samples)  10.5 us
    convert_element_type x2, local copies, waits for them, and re-layouts, shards(): smoothed.astype(jnp.float32) * column_weights  10.5 us
    unnamed x15, local copies, waits for them, and re-layouts  8.91 us
    all_to_all x1, starting transfers between devices, shards(): lax.all_to_all(sample_weight, 'wafer', split_axis=1, concat_axis=0, tiled...  7.84 us
  transfers between devices with their start and end apart: 7, of which 6 were waited for; matrix products, arithmetic and copies ran while one was open for 29% of the time, Pallas kernels for 0%

commit v1 on v0

v1 whole, which is shorter than its diff:
```python
import functools

import jax
import jax.numpy as jnp
from jax import lax
from jax.experimental import pallas as pl
from jax.experimental.pallas import tpu as pltpu
from jax.sharding import PartitionSpec as P

MESH = pl.DeviceIdType.MESH
F32 = jnp.float32
BF16 = jnp.bfloat16


def body(dims, *refs):
    n_tm, n_wf, det, spans, hits, samples, pixels, tiles_own, pack, gather_w = dims
    (ts, sw, whiten, picks, point_in, band, resp, short, hr8, src, ids) = refs[:11]
    out = refs[11]
    (tsb, swb, wsel, wbuf, point, mapb, idb, fs, sig, filt, part, outb, arrb, sums) = refs[12:26]
    (loc, s_ts, r_ts, s_sw, r_sw, s_w1, r_w1, s_w2, r_w2, s_map, r_map, s_id, r_id, s_out, r_out, s_sum, r_sum) = refs[26:]
    t = lax.axis_index("tm")
    w = lax.axis_index("wafer")
    det_own = det // n_wf
    rows = spans * hits
    part_rows = rows * 8
    all_tiles = n_tm * tiles_own

    def tm_to(d):
        return lax.rem(t + d, n_tm)

    def tm_from(d):
        return lax.rem(t + n_tm - d, n_tm)

    def remote(src_ref, dst_ref, send, recv, device):
        return pltpu.make_async_remote_copy(
            src_ref=src_ref, dst_ref=dst_ref, send_sem=send, recv_sem=recv, device_id=device, device_id_type=MESH
        )

    def over_tm(step):
        def run(i, carry):
            step(i + 1)
            return carry

        lax.fori_loop(0, n_tm - 1, run, 0)

    def own_chunk(s):
        cols = pl.ds(pl.multiple_of((w * spans + s) * samples, samples), samples)
        here = pl.ds(pl.multiple_of(w * det_own, det_own), det_own)
        return (
            pltpu.make_async_copy(ts.at[:, cols], tsb.at[s, here, :], loc.at[s]),
            pltpu.make_async_copy(sw.at[:, cols], swb.at[s, here, :], loc.at[spans + s]),
        )

    own_map = pltpu.make_async_copy(short, mapb.at[t], loc.at[2 * spans])
    own_ids = pltpu.make_async_copy(ids.at[t], idb.at[t], loc.at[2 * spans + 1])
    for s in range(spans):
        for copy in own_chunk(s):
            copy.start()
    own_map.start()
    own_ids.start()
    own_point = pltpu.make_async_copy(point_in, point, loc.at[2 * spans + 4])
    own_point.start()
    if gather_w:
        for g in range(n_tm):
            wsel[g] = whiten[picks[g]]
        own_w = pltpu.make_async_copy(wsel.at[t], wbuf.at[t, w], loc.at[2 * spans + 2])
        own_w.start()

    barrier = pltpu.get_barrier_semaphore()

    def greet(d):
        pl.semaphore_signal(barrier, inc=1, device_id=(tm_to(d), w), device_id_type=MESH)

    over_tm(greet)
    for d in range(1, n_wf):
        pl.semaphore_signal(barrier, inc=1, device_id=(t, lax.rem(w + d, n_wf)), device_id_type=MESH)
    pl.semaphore_wait(barrier, n_tm - 1 + n_wf - 1)

    def map_out(d):
        return remote(short, mapb.at[t], s_map.at[d], r_map.at[d], (tm_to(d), w))

    def map_in(d):
        return remote(short, mapb.at[tm_from(d)], s_map.at[d], r_map.at[d], (tm_to(d), w))

    def id_out(d):
        return remote(ids.at[tm_to(d)], idb.at[t], s_id.at[d], r_id.at[d], (tm_to(d), w))

    def id_in(d):
        return remote(ids.at[tm_to(d)], idb.at[tm_from(d)], s_id.at[d], r_id.at[d], (tm_to(d), w))

    def w1_out(d):
        return remote(wsel.at[tm_to(d)], wbuf.at[t, w], s_w1.at[d], r_w1.at[d], (tm_to(d), w))

    def w1_in(d):
        return remote(wsel.at[tm_to(d)], wbuf.at[tm_from(d), w], s_w1.at[d], r_w1.at[d], (tm_to(d), w))

    def chunk(s, d, arriving):
        to = lax.rem(w + d, n_wf)
        row = lax.rem(w + n_wf - d, n_wf) if arriving else w
        cols = pl.ds(pl.multiple_of((to * spans + s) * samples, samples), samples)
        there = pl.ds(pl.multiple_of(row * det_own, det_own), det_own)
        return (
            remote(ts.at[:, cols], tsb.at[s, there, :], s_ts.at[s, d], r_ts.at[s, d], (t, to)),
            remote(sw.at[:, cols], swb.at[s, there, :], s_sw.at[s, d], r_sw.at[s, d], (t, to)),
        )

    def send_span(s):
        for d in range(1, n_wf):
            for copy in chunk(s, d, False):
                copy.start()

    over_tm(lambda d: map_out(d).start())
    if gather_w:
        over_tm(lambda d: w1_out(d).start())
    over_tm(lambda d: id_out(d).start())
    early = spans // 2 if gather_w else spans
    for s in range(early):
        send_span(s)

    own_map.wait()
    over_tm(lambda d: map_in(d).wait_recv())
    at = lax.broadcasted_iota(jnp.int32, (part_rows, all_tiles), 1)
    comp = lax.rem(lax.broadcasted_iota(jnp.int32, (part_rows, all_tiles), 0), 8)
    named = at == hr8[...]
    total = jnp.zeros((part_rows, pixels), F32)
    for j in range(3):
        pick = jnp.where(named & (comp == j), 1.0, 0.0).astype(BF16)
        plane = mapb[:, j].reshape(all_tiles, pixels)
        total += jnp.dot(pick, plane, preferred_element_type=F32)
    fs[...] = total
    own_point.wait()

    if gather_w:
        own_w.wait()
        over_tm(lambda d: w1_in(d).wait_recv())
        mate = w + 1 - 2 * lax.rem(w, 2)
        far = lax.rem(w + 2, n_wf)
        far_mate = far + 1 - 2 * lax.rem(far, 2)

        def w2(kind, arriving):
            who = (mate, far, mate)[kind]
            block = ((mate, far, far_mate) if arriving else (w, w, far))[kind]
            return remote(wbuf.at[:, block], wbuf.at[:, block], s_w2.at[kind], r_w2.at[kind], (t, who))

        w2(1, False).start()
        w2(0, False).start()
        for s in range(early, spans):
            send_span(s)

    def signal_of(c, carry):
        acc = jnp.zeros((8, samples), F32)
        for k in range(hits):
            tile = fs[pl.ds(pl.multiple_of((c * hits + k) * 8, 8), 8), :].astype(BF16)
            acc += lax.dot_general(tile, point[c, k], (((1,), (1,)), ((), ())), preferred_element_type=F32)
        sig[c] = acc
        return carry

    lax.fori_loop(0, spans, signal_of, 0)

    if gather_w:
        w2(1, True).wait_recv()
        w2(2, False).start()
        w2(0, True).wait_recv()
        w2(2, True).wait_recv()

    block = 256
    per_block = block * n_tm // det

    def weights_at(i):
        if gather_w:
            return wbuf[pl.ds(i * per_block, per_block)].reshape(block, det)
        return whiten[pl.ds(pl.multiple_of(i * block, block), block), :]

    def one_span(s, carry):
        for copy in own_chunk(s):
            copy.wait()
        for d in range(1, n_wf):
            for copy in chunk(s, d, True):
                copy.wait_recv()
        srow = sig[s]

        def first(i, carry):
            here = pl.ds(pl.multiple_of(i * block, block), block)
            r = resp[here, :]
            signal = r[:, 0:1] * srow[0:1] + r[:, 1:2] * srow[1:2] + r[:, 2:3] * srow[2:3]
            err = (tsb[s, here, :].astype(F32) - signal) * swb[s, here, :].astype(F32)
            filt[here, :] = jnp.dot(err.astype(BF16), band[...], preferred_element_type=F32).astype(BF16)
            return carry

        lax.fori_loop(0, det // block, first, 0)

        def second(i, acc):
            here = pl.ds(pl.multiple_of(i * block, block), block)
            white = jnp.dot(weights_at(i), filt[...], preferred_element_type=F32).astype(BF16)
            smooth = lax.dot_general(white, band[...], (((1,), (1,)), ((), ())), preferred_element_type=F32)
            x = smooth.astype(BF16).astype(F32) * swb[s, here, :].astype(F32)
            r = resp[here, :]
            return tuple(a + jnp.sum(x * r[:, j : j + 1], axis=0, keepdims=True) for j, a in enumerate(acc))

        zero = jnp.zeros((1, samples), F32)
        acc = lax.fori_loop(0, det // block, second, (zero, zero, zero))
        stokes = jnp.concatenate([*acc, jnp.zeros((5, samples), F32)], axis=0).astype(BF16)
        for k in range(hits):
            there = pl.ds(pl.multiple_of((s * hits + k) * 8, 8), 8)
            part[there, :] = jnp.dot(stokes, point[s, k], preferred_element_type=F32)
        return carry

    lax.fori_loop(0, spans, one_span, 0)

    col = lax.broadcasted_iota(jnp.int32, (n_tm * pack, part_rows), 1)
    place = jnp.where(col == src[...], 1.0, 0.0)
    outb[...] = jnp.dot(place, part[...], preferred_element_type=F32, precision=lax.Precision.HIGHEST).reshape(
        n_tm, pack, pixels
    )
    own_out = pltpu.make_async_copy(outb.at[t], arrb.at[t], loc.at[2 * spans + 3])
    own_out.start()

    def sum_out(d):
        return remote(outb.at[tm_to(d)], arrb.at[t], s_out.at[d], r_out.at[d], (tm_to(d), w))

    def sum_in(d):
        return remote(outb.at[tm_to(d)], arrb.at[tm_from(d)], s_out.at[d], r_out.at[d], (tm_to(d), w))

    over_tm(lambda d: sum_out(d).start())
    own_ids.wait()
    over_tm(lambda d: id_in(d).wait_recv())
    width = 3 * tiles_own
    lanes = idb.shape[2]
    spot = lax.broadcasted_iota(jnp.int32, (n_tm * pack, lanes), 1).astype(F32)
    hit = jnp.where(idb[...].reshape(n_tm * pack, lanes) == spot, 1.0, 0.0)
    own_out.wait()
    over_tm(lambda d: sum_in(d).wait_recv())
    owned = lax.dot_general(
        hit,
        arrb[...].reshape(n_tm * pack, pixels),
        (((0,), (0,)), ((), ())),
        preferred_element_type=F32,
        precision=lax.Precision.HIGHEST,
    )
    sums[w] = owned[:width]

    def share(d, arriving):
        to = lax.rem(w + d, n_wf)
        slot = lax.rem(w + n_wf - d, n_wf) if arriving else w
        return remote(sums.at[w], sums.at[slot], s_sum.at[d], r_sum.at[d], (t, to))

    for d in range(1, n_wf):
        share(d, False).start()
    for d in range(1, n_wf):
        share(d, True).wait_recv()
    result = sums[0]
    for i in range(1, n_wf):
        result = result + sums[i]
    out[...] = result

    def sent(d):
        map_out(d).wait_send()
        id_out(d).wait_send()
        if gather_w:
            w1_out(d).wait_send()
        sum_out(d).wait_send()

    over_tm(sent)
    for d in range(1, n_wf):
        share(d, False).wait_send()

    def spans_sent(s, carry):
        for d in range(1, n_wf):
            for copy in chunk(s, d, False):
                copy.wait_send()
        return carry

    lax.fori_loop(0, spans, spans_sent, 0)
    if gather_w:
        for kind in range(3):
            w2(kind, False).wait_send()


def shards(
    timestream,
    sample_weight,
    response,
    band_filter,
    whiten,
    group_wafer,
    pointing,
    tile_list,
    tile_home,
    solution,
    direction,
    cg_scalars,
):
    n_tm = lax.axis_size("tm")
    n_wf = lax.axis_size("wafer")
    updated = solution + cg_scalars[0] * direction
    tiles_own, comps, pixels = solution.shape
    spans, hits = tile_list.shape
    samples = band_filter.shape[0]
    w_rows, det = whiten.shape[1:]
    rows = spans * hits
    cap = max(2, (rows + n_tm - 1) // n_tm)
    pack = (3 * cap + 7) // 8 * 8
    all_tiles = tile_home.shape[0]
    short = updated.astype(BF16).transpose(1, 0, 2)

    ids_here = tile_list.reshape(rows)
    home = jnp.sum(
        jnp.where(ids_here[:, None] == jnp.arange(all_tiles, dtype=jnp.int32)[None, :], tile_home[None, :], 0), axis=1
    )
    owner = home // tiles_own
    local = home % tiles_own
    order = jnp.arange(rows, dtype=jnp.int32)
    before = jnp.sum(((owner[:, None] == owner[None, :]) & (order[None, :] < order[:, None])).astype(jnp.int32), axis=1)
    m = jnp.arange(n_tm * pack, dtype=jnp.int32)
    slot, comp = (m % pack) // 3, (m % pack) % 3
    match = (
        (owner[None, :] == (m // pack)[:, None]) & (before[None, :] == slot[:, None]) & (slot < cap)[:, None]
    )
    src = jnp.sum(jnp.where(match, order[None, :] * 8 + comp[:, None] + 1, 0), axis=1) - 1
    ids = jnp.sum(jnp.where(match, local[None, :] + comp[:, None] * tiles_own + 1, 0), axis=1) - 1
    lanes = (3 * tiles_own + 127) // 128 * 128
    ids = jnp.broadcast_to(ids.astype(F32).reshape(n_tm, pack, 1), (n_tm, pack, lanes))
    hr8 = jnp.broadcast_to(home[:, None], (rows, 8)).reshape(rows * 8, 1)

    gather_w = w_rows % 16 == 0 and n_wf == 4 and 256 * n_tm % det == 0
    if not gather_w:
        wsel = sum(jnp.where((group_wafer == v)[:, None, None], whiten[v][None], 0) for v in range(whiten.shape[0]))
        mine = lax.all_to_all(wsel, "tm", split_axis=0, concat_axis=0, tiled=True)
        whiten = lax.all_gather(mine, "wafer", axis=1, tiled=True).reshape(det, det)

    any_space = pl.BlockSpec(memory_space=pl.ANY)
    vmem = pl.BlockSpec(memory_space=pltpu.VMEM)
    dma = pltpu.SemaphoreType.DMA
    dims = (n_tm, n_wf, det, spans, hits, samples, pixels, tiles_own, pack, gather_w)
    part_rows = rows * 8
    w_shape = (n_tm, n_wf, w_rows, det) if gather_w else (1, 1, 16, 128)
    summed = pl.pallas_call(
        functools.partial(body, dims),
        out_shape=jax.ShapeDtypeStruct((3 * tiles_own, pixels), F32),
        in_specs=[any_space, any_space, vmem, pl.BlockSpec(memory_space=pltpu.SMEM), any_space] + [vmem] * 6,
        out_specs=vmem,
        scratch_shapes=[
            pltpu.VMEM((spans, det, samples), BF16),
            pltpu.VMEM((spans, det, samples), BF16),
            pltpu.VMEM((n_tm, w_rows, det) if gather_w else (1, 16, 128), BF16),
            pltpu.VMEM(w_shape, BF16),
            pltpu.VMEM(pointing.shape, BF16),
            pltpu.VMEM((n_tm, 3, tiles_own, pixels), BF16),
            pltpu.VMEM((n_tm, pack, lanes), F32),
            pltpu.VMEM((part_rows, pixels), F32),
            pltpu.VMEM((spans, 8, samples), F32),
            pltpu.VMEM((det, samples), BF16),
            pltpu.VMEM((part_rows, pixels), F32),
            pltpu.VMEM((n_tm, pack, pixels), F32),
            pltpu.VMEM((n_tm, pack, pixels), F32),
            pltpu.VMEM((n_wf, 3 * tiles_own, pixels), F32),
            dma((2 * spans + 5,)),
            dma((spans, n_wf)),
            dma((spans, n_wf)),
            dma((spans, n_wf)),
            dma((spans, n_wf)),
            dma((n_tm,)),
            dma((n_tm,)),
            dma((3,)),
            dma((3,)),
            dma((n_tm,)),
            dma((n_tm,)),
            dma((n_tm,)),
            dma((n_tm,)),
            dma((n_tm,)),
            dma((n_tm,)),
            dma((n_wf,)),
            dma((n_wf,)),
        ],
        compiler_params=pltpu.CompilerParams(
            collective_id=0, has_side_effects=True, vmem_limit_bytes=56 * 1024 * 1024
        ),
    )(
        timestream,
        sample_weight,
        whiten,
        group_wafer,
        pointing,
        band_filter,
        response.T,
        short,
        hr8,
        src[:, None],
        ids,
    )
    summed = summed.reshape(3, tiles_own, pixels).transpose(1, 0, 2)
    residual_next = summed * float(det) ** (-0.5)
    direction_next = residual_next + cg_scalars[1] * direction
    return (updated, residual_next, direction_next)


def solution(mesh):
    in_specs = (
        P("wafer", "tm"),
        P("wafer", "tm"),
        P(),
        P(),
        P(None, ("tm", "wafer"), None),
        P(),
        P(("tm", "wafer"), None, None, None),
        P(("tm", "wafer"), None),
        P(),
        P("tm", None, None),
        P("tm", None, None),
        P(),
    )
    out_specs = (P("tm", None, None), P("tm", None, None), P("tm", None, None))
    return jax.shard_map(shards, mesh=mesh, in_specs=in_specs, out_specs=out_specs, check_vma=False)
```

time: 247 us -> 91 us (0.37); the launches traced: 243 us -> 90.7 us
  waiting for transfers between devices: 92.1 us -> 0 us
  Pallas kernels: 0 us -> 78.1 us
  local copies, waits for them, and re-layouts: 67.2 us -> 6.15 us
  matrix products: 30.6 us -> 0 us
  starting transfers between devices: 28 us -> 0 us
  between operations: 16.1 us -> 0.69 us
  other arithmetic: 9.14 us -> 5.68 us
    pallas_call x0 -> x1, Pallas kernels: none -> 78.1 us  [shards(): pl.pallas_call(functools.partial(body, dims), out_shape=jax.ShapeDtypeStr...]
    all_to_all x5 -> x0, waiting for transfers between devices: 63.9 us -> none  [the longest x1 28.7 us: shards(): lax.all_to_all(timestream, 'wafer', split_axis=1, concat_axis=0, tiled=True)]
    convert_element_type x7 -> x1, local copies, waits for them, and re-layouts: 36 us -> 0.08 us  [shards(): ids.astype(F32).reshape(n_tm, pack, 1)]
    dot_general x9 -> x0, matrix products: 30.6 us -> none  [the longest x1 7.15 us: shards(): jnp.einsum('jd,dct->cjt', response, smoothed.astype(jnp.float32) * column...]
    all_to_all x5 -> x0, starting transfers between devices: 27.9 us -> none  [the longest x1 7.84 us: shards(): lax.all_to_all(sample_weight, 'wafer', split_axis=1, concat_axis=0, tiled...]
    psum x1 -> x0, waiting for transfers between devices: 27.5 us -> none  [shards(): summed = lax.psum(owned_sum, 'wafer')]
    reshape x6 -> x1, local copies, waits for them, and re-layouts: 14.5 us -> 0.73 us  [shards(): hr8 = jnp.broadcast_to(home[:, None], (rows, 8)).reshape(rows * 8, 1)]
    unnamed x15 -> x5, local copies, waits for them, and re-layouts: 8.91 us -> 1.74 us
  transfers between devices with their start and end apart: 7 -> 0, of which waited for: 6 -> 0; matrix products, arithmetic and copies ran while one was open for 29% -> 0% of each run, Pallas kernels for 0% -> 0%
where the time goes in v1:
time: 91 us; the launch traced here: 90.7 us
  Pallas kernels  78.1 us (86%)
  local copies, waits for them, and re-layouts  6.15 us (7%)
  other arithmetic  5.68 us (6%)
    pallas_call x1, Pallas kernels, shards(): pl.pallas_call(functools.partial(body, dims), out_shape=jax.ShapeDtypeStr...  78.1 us
    transpose x1, other arithmetic, shards(): short = updated.astype(BF16).transpose(1, 0, 2)  2.29 us

profile of v1, /device:TPU:1, one launch (start us, length us, event | category | flops | bytes accessed | tf_op | source)
XLA Modules:
  0.0 90.7 jit_solution(13909251575621615344)
XLA Ops:
  0.6 0.8 eq.60
  1.4 0.9 select_reduce_fusion
  2.3 1.3 %fusion.1 = (f32[1]{0:T(128)}, f32[1]{0:T(128)}) fusion(f32[2]{0:T(128)} %param.23), kind=kLoop, calls=%fused_computation.29 | loop fusion | bytes 16 | tf_op jit(solution)/shard_map/slice | solution.py:393
  3.6 0.2 convert_reduce_fusion
  3.8 0.1 select_reduce_fusion.1
  3.9 0.1 convert_element_type.19
  4.0 0.1 broadcast_in_dim.23
  4.1 0.7 broadcast_in_dim.25.refs_10_
  4.8 0.7 copy.22.refs_9_
  5.5 0.7 reshape.131.refs_8_
  6.3 2.3 %convert_bitcast_fusion = (bf16[3,32,256]{2,1,0:T(8,128)(2,1)}, f32[32,3,256]{2,0,1:T(8,128)}) fusion(f32[32,3,256]{2,0,1:T(8,128)} %param.21, f32[32,3,256]{2,0,1:T(8,128)} %param.22, f32[]{:T(128)} %bitcast), kind=kLoop, calls=%fused_computation.3 | loop fusion | flops 73728 | bytes 344068 | tf_op jit(solution)/shard_map/transpose | solution.py:304
  8.6 1.7 %copy.20 = f32[3,1024]{0,1:T(8,128)} copy(f32[3,1024]{1,0:T(4,128)} %param.14) | data formatting | bytes 24576 | tf_op args[2]
  10.3 0.0 copy-start.1
  10.3 78.1 %shard_map.139 = f32[96,256]{1,0:T(8,128)} custom-call(bf16[256,4096]{1,0:T(8,128)(2,1)} %refs_0_.1, bf16[256,4096]{1,0:T(8,128)(2,1)} %refs_1_.1, bf16[7,32,1024]{2,1,0:T(8,128)(2,1)} %refs_2_.1, s32[8]{0:T(128)} %refs_3_.1, bf16[4,6,256,256]{3,2,1,0:T(8,128)(2,1)} %refs_4_.1, bf16[256,256]{1,0:T(8,128)(2,1)} %refs_5_.1, f32[1024,3]{1,0:T(8,128)} %bitcast.10, ...), custom_call_target="tpu_custom_call" | custom-call | tf_op jit(solution)/shard_map/pallas_call | solution.py:337
  88.4 0.9 broadcast_multiply_fusion
  89.3 0.0 copy-start
  89.3 0.0 copy-done.1
  89.4 1.3 %multiply_add_fusion = f32[32,3,256]{2,0,1:T(8,128)} fusion(f32[32,3,256]{2,0,1:T(8,128)S(1)} %bitcast.11, f32[32,3,256]{2,0,1:T(8,128)S(1)} %copy-done.1, f32[]{:T(128)} %bitcast.7), kind=kLoop, calls=%fused_computation | loop fusion | flops 49152 | bytes 294916 | tf_op jit(solution)/shard_map/add | solution.py:393
  90.7 0.0 copy-done
  (6 shorter events, 0.1 us)
Async XLA Ops:
  10.3 79.1 %copy-start.1 = (f32[32,3,256]{2,0,1:T(8,128)S(1)}, f32[32,3,256]{2,0,1:T(8,128)}, u32[]{:S(2)}) copy-start(f32[32,3,256]{2,0,1:T(8,128)} %param.22) | copy-start | bytes 294916
  89.3 1.3 %copy-start = (f32[96,256]{1,0:T(8,128)}, f32[96,256]{1,0:T(8,128)S(1)}, u32[]{:S(2)}) copy-start(f32[96,256]{1,0:T(8,128)S(1)} %broadcast_multiply_fusion) | copy-start | bytes 294916
